TPU v7x, 1024 devices: a whole 4x8x16 slice. The times are simulated.
1024 devices in a mesh: gx: 4 (over z_lo), gy: 16 (over z_hi, x), gz: 16 (over y, core).
Axes of the slice: x: 4, y: 8, z: 16 (z_hi: 4, z_lo: 4; z = z_hi * 4 + z_lo), core: 2. Of those that a mesh axis runs over, the one named last changes fastest.
Arguments:
- checkpoint: float32 [19, 32, 128, 512], P(None, 'gz', 'gy', 'gx'), may hold values from -0.067 to 0.734, as said below
- porosity: float32 [32, 128, 512], P('gz', 'gy', 'gx'), may hold values from 0.02 to 0.9
- cell_kind: int32 [32, 128, 512], P('gz', 'gy', 'gx'), may hold values from 0 to 3
- objective_weight: float32 [32, 128, 512], P('gz', 'gy', 'gx'), may hold values from 0.5 to 45
Outputs:
- adjoint_populations: float32 [19, 32, 128, 512], P(None, 'gz', 'gy', 'gx')
- porosity_sensitivity: float32 [32, 128, 512], P('gz', 'gy', 'gx')
- objective: float32 [], replicated
Inputs may be any that keep to these rules, and one draw needn't show every extreme that they name: `cell_kind`: 0 marks fluid, 1 wall, 2 inlet, 3 outlet cells. `checkpoint`: each population is its lattice weight times a factor between -0.2 and 2.2.
All inputs are finite; a program needn't handle non-finite values.
Results may differ from a plain program's by a relative error of at most 0.0003.
Values sent between devices are 32-bit elements; how exact they have to be, the bound alone decides.
No kernel may reach another device: no remote copies, remote signals or barrier semaphores. Data moves between devices by JAX's collectives and lax.ppermute only.
A program may use at most 32 MiB of HBM per device.

v0:
```python
import functools

import jax
import jax.numpy as jnp
import numpy as np
from jax import lax
from jax.experimental import pallas as pl
from jax.experimental.pallas import tpu as pltpu
from jax.sharding import PartitionSpec as P

DIRS = (
    (0, 0, 0),
    (1, 0, 0), (-1, 0, 0), (0, 1, 0), (0, -1, 0), (0, 0, 1), (0, 0, -1),
    (1, 1, 0), (-1, -1, 0), (1, -1, 0), (-1, 1, 0),
    (1, 0, 1), (-1, 0, -1), (1, 0, -1), (-1, 0, 1),
    (0, 1, 1), (0, -1, -1), (0, 1, -1), (0, -1, 1),
)
WEIGHTS = tuple(float(np.float32(w)) for w in [1.0 / 3.0] + [1.0 / 18.0] * 6 + [1.0 / 36.0] * 12)
PAIRS = tuple((i, i + 1) for i in range(1, 19, 2))
RELAX = 1.25
INFLOW = (0.08, 0.0, 0.03)

ZS, YS, XS = 2, 8, 128
HALO = 4
POR, KIND, WGT, FIELDS = 19, 20, 21, 22
SLOTS = XS // (2 * HALO)
EDGE_TILES = -(-FIELDS * ZS // SLOTS)

UP = tuple((c, 0) for c in range(19) if DIRS[c][2] == 1) + tuple(
    (c, 1) for c in range(19) if DIRS[c][2] >= 0
) + ((POR, 1), (KIND, 1))
DOWN = tuple((c, 1) for c in range(19) if DIRS[c][2] == -1) + tuple(
    (c, 0) for c in range(19) if DIRS[c][2] <= 0
) + ((POR, 0), (KIND, 0))
ZMSG = len(UP) + EDGE_TILES


def row_plan(sign, order):
    plan = []
    first = min(order[0], order[1])
    for field in range(FIELDS):
        for z in range(ZS):
            plan.append((field, z, first, 2))
    for z in range(ZS):
        for field in range(WGT):
            if field >= POR or DIRS[field][1] in (0, sign):
                plan.append((field, z, order[2], 1))
    for z in range(ZS):
        for field in range(19):
            if DIRS[field][1] == sign:
                plan.append((field, z, order[3], 1))
    return tuple(plan)


ROWS_LOW = row_plan(-1, (0, 1, 2, 3))
ROWS_HIGH = row_plan(1, (7, 6, 5, 4))
ROWS_MAIN = sum(rows for _, _, _, rows in ROWS_LOW)
ROWS_MSG = -(-(ROWS_MAIN + HALO * EDGE_TILES) // 8) * 8

VMEM_LIMIT = 48 * 1024 * 1024


def rot(value, shift, axis):
    shift = shift % value.shape[axis]
    return value if shift == 0 else pltpu.roll(value, shift, axis)


def lanes():
    return lax.broadcasted_iota(jnp.int32, (YS, XS), 1)


def signed_sum(vector, parts):
    total = None
    for sign, part in zip(vector, parts):
        if sign == 0:
            continue
        if total is None:
            total = part if sign > 0 else -part
        else:
            total = total + part if sign > 0 else total - part
    return total


def momentum(get):
    parts = [None, None, None]
    for plus, minus in PAIRS:
        diff = get(plus) - get(minus)
        for axis in range(3):
            sign = DIRS[plus][axis]
            if sign:
                if parts[axis] is None:
                    parts[axis] = diff if sign > 0 else -diff
                else:
                    parts[axis] = parts[axis] + diff if sign > 0 else parts[axis] - diff
    return parts


def damping(kind, porosity):
    return jnp.where(kind == 2.0, 0.0, 1.0 - porosity)


def damped_of(moment, kind, scale):
    inlet = kind == 3.0
    return [
        scale * part + jnp.where(inlet, level, 0.0) if level else scale * part
        for part, level in zip(moment, INFLOW)
    ]


def post_collision(get, put, density, moment, kind, porosity, masked, wanted=range(19)):
    damped = damped_of(moment, kind, damping(kind, porosity))
    target = jnp.where(kind == 4.0, 1.0, density)
    square = damped[0] * damped[0] + damped[1] * damped[1] + damped[2] * damped[2]
    base = RELAX * (target - 1.5 * square)
    keep = 1.0 - RELAX
    if masked:
        inside = kind > 0.5
        base = jnp.where(inside, base, 0.0)
        damped = [jnp.where(inside, part, 0.0) for part in damped]
        keep = jnp.where(inside, keep, 0.0)
    if 0 in wanted:
        put(0, keep * get(0) + WEIGHTS[0] * base)
    for plus, minus in PAIRS:
        if plus not in wanted and minus not in wanted:
            continue
        weight = WEIGHTS[plus]
        along = signed_sum(DIRS[plus], damped)
        even = weight * base + (4.5 * RELAX * weight) * (along * along)
        odd = (3.0 * RELAX * weight) * along
        if plus in wanted:
            put(plus, keep * get(plus) + (even + odd))
        if minus in wanted:
            put(minus, keep * get(minus) + (even - odd))


def adjoint_collision(get, put, moment, kind, porosity, masked, wanted=range(19)):
    scale = damping(kind, porosity)
    damped = damped_of(moment, kind, scale)
    total = WEIGHTS[0] * get(0)
    slope = [None, None, None]
    for group in (PAIRS[:3], PAIRS[3:]):
        weight = WEIGHTS[group[0][0]]
        even_sum = None
        local = [None, None, None]
        for plus, minus in group:
            first, second = get(plus), get(minus)
            even, odd = first + second, first - second
            even_sum = even if even_sum is None else even_sum + even
            along = signed_sum(DIRS[plus], damped)
            term = odd + 3.0 * (along * even)
            for axis in range(3):
                sign = DIRS[plus][axis]
                if sign:
                    if local[axis] is None:
                        local[axis] = term if sign > 0 else -term
                    else:
                        local[axis] = local[axis] + term if sign > 0 else local[axis] - term
        total = total + weight * even_sum
        slope = [
            weight * new if old is None else old + weight * new for old, new in zip(slope, local)
        ]
    slope = [(3.0 * RELAX) * (part - total * drift) for part, drift in zip(slope, damped)]
    dot = slope[0] * moment[0] + slope[1] * moment[1] + slope[2] * moment[2]
    share = jnp.where(kind == 2.0, 0.0, -dot)
    even = jnp.where(kind == 4.0, 0.0, RELAX * total)
    back = [scale * part for part in slope]
    keep = 1.0 - RELAX
    if masked:
        inside = kind > 0.5
        even = jnp.where(inside, even, 0.0)
        back = [jnp.where(inside, part, 0.0) for part in back]
        keep = jnp.where(inside, keep, 0.0)
    if 0 in wanted:
        put(0, keep * get(0) + even)
    for plus, minus in PAIRS:
        if plus not in wanted and minus not in wanted:
            continue
        along = signed_sum(DIRS[plus], back)
        if plus in wanted:
            put(plus, keep * get(plus) + (even + along))
        if minus in wanted:
            put(minus, keep * get(minus) + (even - along))
    return share


def parity(axis):
    return lax.axis_index(axis) % 2 == 1


def edges_kernel(f_hbm, por_hbm, kind_hbm, wgt_hbm, state_ref, edge_ref, f_ref, por_ref, kind_ref, wgt_ref, sems):
    copies = [
        pltpu.make_async_copy(source, target, sems.at[at])
        for at, (source, target) in enumerate(
            ((f_hbm, f_ref), (por_hbm, por_ref), (kind_hbm, kind_ref), (wgt_hbm, wgt_ref))
        )
    ]
    for copy in copies:
        copy.start()
    for copy in copies:
        copy.wait()
    for z in range(ZS):
        get = lambda i: f_ref[i, z]
        density = functools.reduce(lambda a, b: a + b, [get(i) for i in range(19)])
        kind = kind_ref[z].astype(jnp.float32) + 1.0

        def put(i, value):
            state_ref[i, z] = value

        post_collision(get, put, density, momentum(get), kind, por_ref[z], False)
        state_ref[POR, z] = por_ref[z]
        state_ref[KIND, z] = kind
        state_ref[WGT, z] = wgt_ref[z]
    slot_of = lanes() // (2 * HALO)
    for tile in range(EDGE_TILES):
        packed = jnp.zeros((YS, XS), jnp.float32)
        for slot in range(SLOTS):
            field, z = divmod(tile * SLOTS + slot, ZS)
            if field < FIELDS:
                moved = rot(state_ref[field, z], 2 * HALO * slot + HALO, 1)
                packed = jnp.where(slot_of == slot, moved, packed)
        edge_ref[tile] = packed


def rows_kernel(state_ref, odd_ref, even_ref, edge_ref, to_odd_ref, to_even_ref):
    from_left = (lanes() % (2 * HALO) < HALO).astype(jnp.int32)
    mine = (lax.axis_index("gx") % 2).astype(jnp.int32)
    for tile in range(EDGE_TILES):
        edge_ref[tile] = jnp.where(from_left == mine, even_ref[tile], odd_ref[tile])

    def pack(plan, start, ref):
        at = 0
        for field, z, row, rows in plan:
            ref[at : at + rows] = state_ref[field, z, row : row + rows]
            at += rows
        for tile in range(EDGE_TILES):
            at = ROWS_MAIN + HALO * tile
            ref[at : at + HALO] = edge_ref[tile, start : start + HALO]

    odd = parity("gy")

    @pl.when(odd)
    def _():
        pack(ROWS_LOW, 0, to_even_ref)
        pack(ROWS_HIGH, HALO, to_odd_ref)

    @pl.when(jnp.logical_not(odd))
    def _():
        pack(ROWS_HIGH, HALO, to_even_ref)
        pack(ROWS_LOW, 0, to_odd_ref)


def planes_kernel(state_ref, edge_ref, odd_ref, even_ref, wide_ref, side_ref, to_odd_ref, to_even_ref):
    for field in range(FIELDS):
        for z in range(ZS):
            wide_ref[field, z, 0] = state_ref[field, z]
    for tile in range(EDGE_TILES):
        side_ref[tile, 0] = edge_ref[tile]

    def unpack(plan, start, ref):
        at = 0
        for field, z, row, rows in plan:
            wide_ref[field, z, 1, row : row + rows] = ref[at : at + rows]
            at += rows
        for tile in range(EDGE_TILES):
            at = ROWS_MAIN + HALO * tile
            side_ref[tile, 1, start : start + HALO] = ref[at : at + HALO]

    odd = parity("gy")

    @pl.when(odd)
    def _():
        unpack(ROWS_HIGH, HALO, even_ref)
        unpack(ROWS_LOW, 0, odd_ref)

    @pl.when(jnp.logical_not(odd))
    def _():
        unpack(ROWS_LOW, 0, even_ref)
        unpack(ROWS_HIGH, HALO, odd_ref)

    def pack(plan, ref):
        for at, (field, z) in enumerate(plan):
            ref[at] = wide_ref[field, z]
        for tile in range(EDGE_TILES):
            ref[len(plan) + tile] = side_ref[tile]

    odd_z = parity("gz")

    @pl.when(odd_z)
    def _():
        pack(DOWN, to_even_ref)
        pack(UP, to_odd_ref)

    @pl.when(jnp.logical_not(odd_z))
    def _():
        pack(UP, to_even_ref)
        pack(DOWN, to_odd_ref)


def join(main, packed, slot):
    main = main.reshape(2 * YS, XS)
    side = rot(packed.reshape(2 * YS, XS), XS - HALO - 2 * HALO * slot, 1)
    return jnp.concatenate([main, side], axis=1)


def forward_kernel(scale, wide_ref, side_ref, odd_ref, even_ref, aux_ref, flow_ref, part_ref, f_ref):
    odd = parity("gz")

    def field_at(field, z):
        own = z % ZS
        tile, slot = divmod(field * ZS + own, SLOTS)
        if 0 <= z < ZS:
            return join(wide_ref[field, z], side_ref[tile], slot)
        plan = UP if z < 0 else DOWN
        main, side = plan.index((field, own)), len(plan) + tile
        first, second = (even_ref, odd_ref) if z < 0 else (odd_ref, even_ref)
        return join(
            jnp.where(odd, first[main], second[main]),
            jnp.where(odd, first[side], second[side]),
            slot,
        )

    for z in range(-1, ZS + 1):
        at = z + 1
        density = None
        moment = [None, None, None]
        for c in range(19):
            cx, cy, cz = DIRS[c]
            value = rot(rot(field_at(c, z - cz), cy, 0), cx, 1)
            f_ref[c, at] = value
            density = value if density is None else density + value
        get = lambda i: f_ref[i, at]
        moment = momentum(get)
        porosity, kind = field_at(POR, z), field_at(KIND, z)
        for axis in range(3):
            aux_ref[axis, at] = moment[axis]
        aux_ref[3, at] = porosity
        aux_ref[4, at] = kind

        def put(i, value):
            f_ref[i, at] = value

        wanted = [i for i in range(1, 19) if 0 <= z + DIRS[i][2] < ZS]
        post_collision(get, put, density, moment, kind, porosity, True, wanted)

    partial = jnp.zeros((YS, XS), jnp.float32)
    slot_of = lax.broadcasted_iota(jnp.int32, (2 * YS, XS), 1) // (2 * HALO)
    packed = jnp.zeros((2 * YS, XS), jnp.float32)
    for z in range(ZS):
        def arrived(i):
            cx, cy, cz = DIRS[i]
            return rot(rot(f_ref[i, z - cz + 1], cy, 0), cx, 1)

        moment = momentum(arrived)
        weight = field_at(WGT, z)
        for axis in range(3):
            flow = weight * moment[axis]
            partial = partial + flow[:YS, :XS] * moment[axis][:YS, :XS]
            slot = axis * ZS + z
            flow_ref[slot] = flow[:, :XS].reshape(2, YS, XS)
            moved = rot(flow[:, XS:], 2 * HALO * slot + HALO, 1)
            packed = jnp.where(slot_of == slot, moved, packed)
    flow_ref[3 * ZS] = packed.reshape(2, YS, XS)
    total = scale * jnp.sum(partial, axis=0, keepdims=True)
    part_ref[...] = jnp.broadcast_to(total[None], part_ref.shape)


def backward_kernel(
    flow_ref, even_ref, odd_ref, aux_ref, f_ref, por_ref, kind_ref, adjoint_ref, share_ref, g_ref
):
    odd = parity("gz")

    def flow_at(axis, z):
        slot = axis * ZS + z % ZS
        if 0 <= z < ZS:
            return join(flow_ref[slot], flow_ref[3 * ZS], slot)
        first, second = (even_ref, odd_ref) if z < 0 else (odd_ref, even_ref)
        return join(
            jnp.where(odd, first[slot], second[slot]),
            jnp.where(odd, first[3 * ZS], second[3 * ZS]),
            slot,
        )

    flows = [[flow_at(axis, z) for axis in range(3)] for z in range(-2, ZS + 2)]
    shares = []
    for z in range(-1, ZS + 1):
        at = z + 1
        g_ref[0, at] = jnp.zeros((2 * YS, 2 * XS), jnp.float32)
        for i in range(1, 19):
            cx, cy, cz = DIRS[i]
            seed = signed_sum(DIRS[i], flows[z + cz + 2])
            g_ref[i, at] = rot(rot(seed, -cy, 0), -cx, 1)
        get = lambda i: g_ref[i, at]

        def put(i, value):
            g_ref[i, at] = value

        moment = [aux_ref[axis, at] for axis in range(3)]
        wanted = [i for i in range(19) if 0 <= z - DIRS[i][2] < ZS]
        share = adjoint_collision(get, put, moment, aux_ref[4, at], aux_ref[3, at], True, wanted)
        if 0 <= z < ZS:
            shares.append(share[:YS, :XS])
    for z in range(ZS):
        for i in range(19):
            cx, cy, cz = DIRS[i]
            value = rot(g_ref[i, z + cz + 1], -cy, 0)[:YS]
            adjoint_ref[i, z] = rot(value, -cx, 1)[:, :XS]
        carried = lambda i: adjoint_ref[i, z]

        def put_out(i, value):
            adjoint_ref[i, z] = value

        moment = momentum(lambda i: f_ref[i, z])
        kind = kind_ref[z].astype(jnp.float32) + 1.0
        share = adjoint_collision(carried, put_out, moment, kind, por_ref[z], False)
        share_ref[z] = shares[z] + share


def spread_kernel(in_ref, out_ref):
    out_ref[...] = jnp.broadcast_to(jnp.sum(in_ref[...], axis=0, keepdims=True), out_ref.shape)


def call(kernel, outs, scratch=(), **options):
    shapes = tuple(jax.ShapeDtypeStruct(shape, jnp.float32) for shape in outs)
    return pl.pallas_call(
        kernel,
        out_shape=shapes if len(shapes) > 1 else shapes[0],
        scratch_shapes=[
            pltpu.VMEM(shape, jnp.float32) if isinstance(shape, tuple) else shape for shape in scratch
        ],
        compiler_params=pltpu.CompilerParams(vmem_limit_bytes=VMEM_LIMIT),
        **options,
    )


def swap(axis, to_even, to_odd, even_first=False):
    count = lax.axis_size(axis)

    def partners(first):
        return [
            pair for low in range(first, count - 1, 2) for pair in ((low, low + 1), (low + 1, low))
        ]

    if even_first:
        even = lax.ppermute(to_even, axis, partners(0))
        odd = lax.ppermute(to_odd, axis, partners(1))
    else:
        odd = lax.ppermute(to_odd, axis, partners(1))
        even = lax.ppermute(to_even, axis, partners(0))
    return odd, even


def columns():
    sizes = [lax.axis_size(axis) for axis in ("gx", "gy", "gz")]
    places = [(x, y) for x in range(sizes[0]) for y in range(sizes[1])]
    places.sort(key=lambda place: (place[1] // 4 * sizes[0] + place[0], place[1] % 4), reverse=True)
    turn = len(places) // 8
    places = places[turn:] + places[:turn]
    return [[(x * sizes[1] + y) * sizes[2] + z for x, y in places] for z in range(sizes[2])]


def per_device(checkpoint, porosity, cell_kind, objective_weight):
    brick = (ZS, YS, XS)
    state, edge = call(
        edges_kernel,
        [(FIELDS,) + brick, (EDGE_TILES, YS, XS)],
        [(19,) + brick, brick, pltpu.VMEM(brick, jnp.int32), brick, pltpu.SemaphoreType.DMA((4,))],
        in_specs=[pl.BlockSpec(memory_space=pl.ANY)] * 4,
    )(
        *(
            pltpu.with_memory_space_constraint(value, pltpu.HBM)
            for value in (checkpoint, porosity, cell_kind, objective_weight)
        )
    )
    rows = (ROWS_MSG, XS)
    edge, to_odd, to_even = call(rows_kernel, [(EDGE_TILES, YS, XS), rows, rows])(
        state, *swap("gx", edge, edge)
    )
    planes = (ZMSG, 2, YS, XS)
    wide, side, to_odd, to_even = call(
        planes_kernel, [(FIELDS, ZS, 2, YS, XS), (EDGE_TILES, 2, YS, XS), planes, planes]
    )(state, edge, *swap("gy", to_even, to_odd))
    field = (ZS + 2, 2 * YS, 2 * XS)
    group = lax.axis_size("gz")
    plane = lax.axis_size("gx") * lax.axis_size("gy")
    cells = group * plane * ZS * YS * XS
    aux, flow, part = call(
        functools.partial(forward_kernel, 0.5 / cells),
        [(5,) + field, (3 * ZS + 1, 2, YS, XS), (group, 1, XS)],
        [(19,) + field],
    )(wide, side, *swap("gz", to_even, to_odd))
    flow_odd, flow_even = swap("gz", flow, flow, True)
    part = lax.all_to_all(part, "gz", 0, 0, tiled=True)
    part = call(spread_kernel, [(plane, 1, XS)])(part)
    part = lax.all_to_all(
        part, ("gx", "gy", "gz"), 0, 0, axis_index_groups=columns(), tiled=True
    )
    objective = jnp.sum(part)
    adjoint, share = call(backward_kernel, [(19,) + brick, brick], [(19,) + field])(
        flow, flow_even, flow_odd, aux, checkpoint, porosity, cell_kind
    )
    return adjoint, share, objective


def solution(mesh):
    cells = P("gz", "gy", "gx")
    populations = P(None, "gz", "gy", "gx")
    return jax.shard_map(
        per_device,
        mesh=mesh,
        in_specs=(populations, cells, cells, cells),
        out_specs=(populations, cells, P()),
        check_vma=False,
    )
```

profile of v0, /device:TPU:1, one launch (start us, length us, event | category | flops | bytes accessed | tf_op | source)
XLA Modules:
  0.0 81.4 jit_solution(3422281118339247770)
XLA Ops:
  0.6 1.1 %shard_map.67 = (f32[22,2,8,128]{3,2,1,0:T(8,128)S(1)}, f32[3,8,128]{2,1,0:T(8,128)S(1)}) custom-call(f32[19,2,8,128]{3,2,1,0:T(8,128)} %f_ref.1, f32[2,8,128]{2,1,0:T(8,128)} %por_ref.1, s32[2,8,128]{2,1,0:T(8,128)} %kind_ref.1, f32[2,8,128]{2,1,0:T(8,128)} %wgt_hbm.1), custom_call_target="tpu_custom_call" | custom-call | tf_op jit(solution)/shard_map/pallas_call | solution.py:463
  1.7 4.8 %collective-permute-start.1 = (f32[3,8,128]{2,1,0:T(8,128)S(1)}, f32[3,8,128]{2,1,0:T(8,128)S(1)}, u32[]{:S(2)}, u32[]{:S(2)}) collective-permute-start(f32[3,8,128]{2,1,0:T(8,128)S(1)} %get-tuple-element.18), channel_id=1, source_target_pairs={{0,256},{256,0},{512,768},{768,512},{1,257},{257,1},{513,769},{769... | collective-permute-start | bytes 36872 | tf_op jit(solution)/shard_map/ppermute | solution.py:448
  6.6 0.7 collective-permute-start
  7.2 0.4 collective-permute-done.1.even_ref
  7.6 0.0 collective-permute-done.odd_ref
  7.6 0.1 shard_map.68
  7.7 0.7 collective-permute-start.2
  8.4 5.6 %collective-permute-start.3 = (f32[144,128]{1,0:T(8,128)S(1)}, f32[144,128]{1,0:T(8,128)S(1)}, u32[]{:S(2)}, u32[]{:S(2)}) collective-permute-start(f32[144,128]{1,0:T(8,128)S(1)} %get-tuple-element.21), channel_id=1, source_target_pairs={{0,16},{16,0},{32,48},{48,32},{64,80},{80,64},{96,112},{112,96},{1... | collective-permute-start | bytes 221192 | tf_op jit(solution)/shard_map/ppermute | solution.py:448
  14.0 0.0 collective-permute-done.2.odd_ref
  14.0 1.7 %collective-permute-done.3.even_ref = f32[144,128]{1,0:T(8,128)S(1)} collective-permute-done((f32[144,128]{1,0:T(8,128)S(1)}, f32[144,128]{1,0:T(8,128)S(1)}, u32[]{:S(2)}, u32[]{:S(2)}) %collective-permute-start.3) | collective-permute-done | bytes 73760 | tf_op jit(solution)/shard_map/ppermute | solution.py:448
  15.7 0.1 shard_map.69
  15.8 5.8 %collective-permute-start.4 = (f32[24,2,8,128]{3,2,1,0:T(8,128)S(1)}, f32[24,2,8,128]{3,2,1,0:T(8,128)S(1)}, u32[]{:S(2)}, u32[]{:S(2)}) collective-permute-start(f32[24,2,8,128]{3,2,1,0:T(8,128)S(1)} %get-tuple-element.24), channel_id=1, source_target_pairs={{1,2},{2,1},{3,4},{4,3},{5,6},{6,5},{7,8},{8,7},{9,10},{10,9},{11,... | collective-permute-start | bytes 589832 | tf_op jit(solution)/shard_map/ppermute | solution.py:447
  21.6 9.6 %collective-permute-start.5 = (f32[24,2,8,128]{3,2,1,0:T(8,128)S(1)}, f32[24,2,8,128]{3,2,1,0:T(8,128)S(1)}, u32[]{:S(2)}, u32[]{:S(2)}) collective-permute-start(f32[24,2,8,128]{3,2,1,0:T(8,128)S(1)} %get-tuple-element.25), channel_id=1, source_target_pairs={{0,1},{1,0},{2,3},{3,2},{4,5},{5,4},{6,7},{7,6},{8,9},{9,8},{10,11... | collective-permute-start | bytes 589832 | tf_op jit(solution)/shard_map/ppermute | solution.py:448
  31.2 0.0 collective-permute-done.4.odd_ref
  31.2 1.0 %collective-permute-done.5.even_ref = f32[24,2,8,128]{3,2,1,0:T(8,128)S(1)} collective-permute-done((f32[24,2,8,128]{3,2,1,0:T(8,128)S(1)}, f32[24,2,8,128]{3,2,1,0:T(8,128)S(1)}, u32[]{:S(2)}, u32[]{:S(2)}) %collective-permute-start.5) | collective-permute-done | bytes 196640 | tf_op jit(solution)/shard_map/ppermute | solution.py:448
  32.3 0.0 copy-start
  32.3 2.1 %shard_map.70 = (f32[5,4,16,256]{3,2,1,0:T(8,128)S(1)}, f32[7,2,8,128]{3,2,1,0:T(8,128)S(1)}, f32[16,1,128]{2,1,0:T(1,128)S(1)}) custom-call(f32[22,2,2,8,128]{4,3,2,1,0:T(8,128)S(1)} %get-tuple-element.22.wide_ref, f32[3,2,8,128]{3,2,1,0:T(8,128)S(1)} %get-tuple-element.23.side_ref, f32[24,2,8,128]{3,2,1,0:T(8,128)S(1)} %collective-permute-done.4.odd_ref, ...), custom_call_target="tpu_custom_call" | custom-call | tf_op jit(solution)/shard_map/pallas_call | solution.py:486
  34.4 9.8 %all_to_all.10.in_ref = f32[16,1,128]{2,1,0:T(1,128)S(1)} all-to-all(f32[16,1,128]{2,1,0:T(1,128)S(1)} %get-tuple-element.30), channel_id=1, replica_groups=mesh['gx'=4,'gy'=16,'gz'=16] {'gz'}, dimensions={0} | all-to-all | bytes 16384 | tf_op jit(solution)/shard_map/all_to_all | solution.py:492
  44.2 0.6 shard_map.72
  44.8 0.0 copy-start.1
  44.8 0.0 copy-start.2
  44.8 27.8 %all-to-all-start.1 = ((f32[64,1,128]{2,1,0:T(1,128)}), f32[64,1,128]{2,1,0:T(1,128)S(1)}, u32[]{:S(2)}, u32[]{:S(2)}) async-start(f32[64,1,128]{2,1,0:T(1,128)} %shard_map.72), calls=%async_computation.1 | async-start | bytes 65536 | tf_op jit(solution)/shard_map/all_to_all | solution.py:494
  72.7 3.3 %collective-permute-start.7 = (f32[7,2,8,128]{3,2,1,0:T(8,128)S(1)}, f32[7,2,8,128]{3,2,1,0:T(8,128)S(1)}, u32[]{:S(2)}, u32[]{:S(2)}) collective-permute-start(f32[7,2,8,128]{3,2,1,0:T(8,128)S(1)} %get-tuple-element.26.flow_ref), channel_id=1, source_target_pairs={{1,2},{2,1},{3,4},{4,3},{5,6},{6,5},{7,8},{8,7},{9,10},{10,9},{11,... | collective-permute-start | bytes 172040 | tf_op jit(solution)/shard_map/ppermute | solution.py:445
  75.9 1.9 %collective-permute-start.6 = (f32[7,2,8,128]{3,2,1,0:T(8,128)S(1)}, f32[7,2,8,128]{3,2,1,0:T(8,128)S(1)}, u32[]{:S(2)}, u32[]{:S(2)}) collective-permute-start(f32[7,2,8,128]{3,2,1,0:T(8,128)S(1)} %get-tuple-element.26.flow_ref), channel_id=1, source_target_pairs={{0,1},{1,0},{2,3},{3,2},{4,5},{5,4},{6,7},{7,6},{8,9},{9,8},{10,11... | collective-permute-start | bytes 172040 | tf_op jit(solution)/shard_map/ppermute | solution.py:444
  77.9 0.6 collective-permute-done.7.odd_ref
  78.4 0.6 collective-permute-done.6.even_ref
  79.1 0.0 copy-done
  79.1 0.0 copy-done.1
  79.1 0.0 copy-done.2
  79.1 1.2 %shard_map.71 = (f32[19,2,8,128]{3,2,1,0:T(8,128)}, f32[2,8,128]{2,1,0:T(8,128)}) custom-call(f32[7,2,8,128]{3,2,1,0:T(8,128)S(1)} %get-tuple-element.26.flow_ref, f32[7,2,8,128]{3,2,1,0:T(8,128)S(1)} %collective-permute-done.6.even_ref, f32[7,2,8,128]{3,2,1,0:T(8,128)S(1)} %collective-permute-done.7.odd_ref, ...), custom_call_target="tpu_custom_call" | custom-call | tf_op jit(solution)/shard_map/pallas_call | solution.py:498
  80.3 0.5 all-to-all-done.1
  80.8 0.7 reduce_sum.9
Async XLA Ops:
  1.7 5.9 %collective-permute-start.1 = (f32[3,8,128]{2,1,0:T(8,128)S(1)}, f32[3,8,128]{2,1,0:T(8,128)S(1)}, u32[]{:S(2)}, u32[]{:S(2)}) collective-permute-start(f32[3,8,128]{2,1,0:T(8,128)S(1)} %get-tuple-element.18), channel_id=1, source_target_pairs={{0,256},{256,0},{512,768},{768,512},{1,257},{257,1},{513,769},{769... | collective-permute-start | bytes 36872 | tf_op jit(solution)/shard_map/ppermute | solution.py:448
  6.6 1.1 %collective-permute-start = (f32[3,8,128]{2,1,0:T(8,128)S(1)}, f32[3,8,128]{2,1,0:T(8,128)S(1)}, u32[]{:S(2)}, u32[]{:S(2)}) collective-permute-start(f32[3,8,128]{2,1,0:T(8,128)S(1)} %get-tuple-element.18), channel_id=1, source_target_pairs={{256,512},{512,256},{257,513},{513,257},{258,514},{514,258},{259,5... | collective-permute-start | bytes 36872 | tf_op jit(solution)/shard_map/ppermute | solution.py:447
  7.7 6.3 %collective-permute-start.2 = (f32[144,128]{1,0:T(8,128)S(1)}, f32[144,128]{1,0:T(8,128)S(1)}, u32[]{:S(2)}, u32[]{:S(2)}) collective-permute-start(f32[144,128]{1,0:T(8,128)S(1)} %get-tuple-element.20), channel_id=1, source_target_pairs={{16,32},{32,16},{48,64},{64,48},{80,96},{96,80},{112,128},{128,112... | collective-permute-start | bytes 221192 | tf_op jit(solution)/shard_map/ppermute | solution.py:447
  8.4 7.3 %collective-permute-start.3 = (f32[144,128]{1,0:T(8,128)S(1)}, f32[144,128]{1,0:T(8,128)S(1)}, u32[]{:S(2)}, u32[]{:S(2)}) collective-permute-start(f32[144,128]{1,0:T(8,128)S(1)} %get-tuple-element.21), channel_id=1, source_target_pairs={{0,16},{16,0},{32,48},{48,32},{64,80},{80,64},{96,112},{112,96},{1... | collective-permute-start | bytes 221192 | tf_op jit(solution)/shard_map/ppermute | solution.py:448
  15.8 15.4 %collective-permute-start.4 = (f32[24,2,8,128]{3,2,1,0:T(8,128)S(1)}, f32[24,2,8,128]{3,2,1,0:T(8,128)S(1)}, u32[]{:S(2)}, u32[]{:S(2)}) collective-permute-start(f32[24,2,8,128]{3,2,1,0:T(8,128)S(1)} %get-tuple-element.24), channel_id=1, source_target_pairs={{1,2},{2,1},{3,4},{4,3},{5,6},{6,5},{7,8},{8,7},{9,10},{10,9},{11,... | collective-permute-start | bytes 589832 | tf_op jit(solution)/shard_map/ppermute | solution.py:447
  21.6 10.6 %collective-permute-start.5 = (f32[24,2,8,128]{3,2,1,0:T(8,128)S(1)}, f32[24,2,8,128]{3,2,1,0:T(8,128)S(1)}, u32[]{:S(2)}, u32[]{:S(2)}) collective-permute-start(f32[24,2,8,128]{3,2,1,0:T(8,128)S(1)} %get-tuple-element.25), channel_id=1, source_target_pairs={{0,1},{1,0},{2,3},{3,2},{4,5},{5,4},{6,7},{7,6},{8,9},{9,8},{10,11... | collective-permute-start | bytes 589832 | tf_op jit(solution)/shard_map/ppermute | solution.py:448
  32.3 46.8 %copy-start = (f32[19,2,8,128]{3,2,1,0:T(8,128)S(1)}, f32[19,2,8,128]{3,2,1,0:T(8,128)}, u32[]{:S(2)}) copy-start(f32[19,2,8,128]{3,2,1,0:T(8,128)} %f_ref.1) | copy-start | bytes 466948
  44.8 34.3 %copy-start.1 = (f32[2,8,128]{2,1,0:T(8,128)S(1)}, f32[2,8,128]{2,1,0:T(8,128)}, u32[]{:S(2)}) copy-start(f32[2,8,128]{2,1,0:T(8,128)} %por_ref.1) | copy-start | bytes 24580
  44.8 34.3 %copy-start.2 = (s32[2,8,128]{2,1,0:T(8,128)S(1)}, s32[2,8,128]{2,1,0:T(8,128)}, u32[]{:S(2)}) copy-start(s32[2,8,128]{2,1,0:T(8,128)} %kind_ref.1) | copy-start | bytes 24580
  44.8 35.9 %all-to-all-start.1 = ((f32[64,1,128]{2,1,0:T(1,128)}), f32[64,1,128]{2,1,0:T(1,128)S(1)}, u32[]{:S(2)}, u32[]{:S(2)}) async-start(f32[64,1,128]{2,1,0:T(1,128)} %shard_map.72), calls=%async_computation.1 | async-start | bytes 65536 | tf_op jit(solution)/shard_map/all_to_all | solution.py:494
  72.7 5.8 %collective-permute-start.7 = (f32[7,2,8,128]{3,2,1,0:T(8,128)S(1)}, f32[7,2,8,128]{3,2,1,0:T(8,128)S(1)}, u32[]{:S(2)}, u32[]{:S(2)}) collective-permute-start(f32[7,2,8,128]{3,2,1,0:T(8,128)S(1)} %get-tuple-element.26.flow_ref), channel_id=1, source_target_pairs={{1,2},{2,1},{3,4},{4,3},{5,6},{6,5},{7,8},{8,7},{9,10},{10,9},{11,... | collective-permute-start | bytes 172040 | tf_op jit(solution)/shard_map/ppermute | solution.py:445
  75.9 3.1 %collective-permute-start.6 = (f32[7,2,8,128]{3,2,1,0:T(8,128)S(1)}, f32[7,2,8,128]{3,2,1,0:T(8,128)S(1)}, u32[]{:S(2)}, u32[]{:S(2)}) collective-permute-start(f32[7,2,8,128]{3,2,1,0:T(8,128)S(1)} %get-tuple-element.26.flow_ref), channel_id=1, source_target_pairs={{0,1},{1,0},{2,3},{3,2},{4,5},{5,4},{6,7},{7,6},{8,9},{9,8},{10,11... | collective-permute-start | bytes 172040 | tf_op jit(solution)/shard_map/ppermute | solution.py:444
where the time goes:
time: 81.9 us; the launch traced here: 81.4 us
  starting transfers between devices  60.1 us (73%)
  blocking collectives  9.82 us (12%)
  Pallas kernels  5.23 us (6%)
  waiting for transfers between devices  4.85 us (6%)
    all_to_all x1, starting transfers between devices, per_device(): lax.all_to_all(part, ('gx', 'gy', 'gz'), 0, 0, axis_index_groups=columns(...  27.8 us
    ppermute x4, starting transfers between devices, swap(): even = lax.ppermute(to_even, axis, partners(0))  21.9 us
    ppermute x4, starting transfers between devices, swap(): odd = lax.ppermute(to_odd, axis, partners(1))  10.4 us
    all_to_all x1, blocking collectives, per_device(): part = lax.all_to_all(part, 'gz', 0, 0, tiled=True)  9.82 us
    ppermute x4, waiting for transfers between devices, swap(): even = lax.ppermute(to_even, axis, partners(0))  3.79 us
    pallas_call x1, Pallas kernels, per_device(): call(functools.partial(forward_kernel, 0.5 / cells), [(5,) + field, (3 *...  2.11 us
  transfers between devices with their start and end apart: 9, of which 6 were waited for; matrix products, arithmetic and copies ran while one was open for 0% of the time, Pallas kernels for 1%

commit v1 on v0

--- a/solution.py
+++ b/solution.py
@@ -489,7 +489,8 @@
         [(19,) + field],
     )(wide, side, *swap("gz", to_even, to_odd))
     flow_odd, flow_even = swap("gz", flow, flow, True)
-    part = lax.all_to_all(part, "gz", 0, 0, tiled=True)
+    falling = [list(range(group))[::-1]]
+    part = lax.all_to_all(part, "gz", 0, 0, axis_index_groups=falling, tiled=True)
     part = call(spread_kernel, [(plane, 1, XS)])(part)
     part = lax.all_to_all(
         part, ("gx", "gy", "gz"), 0, 0, axis_index_groups=columns(), tiled=True

time: 81.9 us -> 79.5 us (0.971)
  starting transfers between devices: 60.1 us -> 58.8 us
  blocking collectives: 9.82 us -> 8.78 us
    all_to_all x1, starting transfers between devices: 27.8 us -> 26.5 us  [per_device(): lax.all_to_all(part, ('gx', 'gy', 'gz'), 0, 0, axis_index_groups=columns(...]
    all_to_all x1, blocking collectives: 9.82 us -> 8.78 us  [per_device(): lax.all_to_all(part, 'gz', 0, 0, axis_index_groups=falling, tiled=True)]
  transfers between devices with their start and end apart: 9 -> 9, of which waited for: 6 -> 6; matrix products, arithmetic and copies ran while one was open for 0% -> 0% of each run, Pallas kernels for 1% -> 2%
where the time goes in v1:
time: 79.5 us; the launch traced here: 79.1 us
  starting transfers between devices  58.8 us (74%)
  blocking collectives  8.78 us (11%)
  Pallas kernels  5.23 us (7%)
  waiting for transfers between devices  4.81 us (6%)
    all_to_all x1, starting transfers between devices, per_device(): lax.all_to_all(part, ('gx', 'gy', 'gz'), 0, 0, axis_index_groups=columns(...  26.5 us
    ppermute x4, starting transfers between devices, swap(): even = lax.ppermute(to_even, axis, partners(0))  21.9 us
    ppermute x4, starting transfers between devices, swap(): odd = lax.ppermute(to_odd, axis, partners(1))  10.4 us
    all_to_all x1, blocking collectives, per_device(): lax.all_to_all(part, 'gz', 0, 0, axis_index_groups=falling, tiled=True)  8.78 us
    ppermute x4, waiting for transfers between devices, swap(): even = lax.ppermute(to_even, axis, partners(0))  3.82 us
    pallas_call x1, Pallas kernels, per_device(): call(functools.partial(forward_kernel, 0.5 / cells), [(5,) + field, (3 *...  2.11 us
  transfers between devices with their start and end apart: 9, of which 6 were waited for; matrix products, arithmetic and copies ran while one was open for 0% of the time, Pallas kernels for 2%

profile of v1, /device:TPU:1, one launch (start us, length us, event | category | flops | bytes accessed | tf_op | source)
XLA Modules:
  0.0 79.1 jit_solution(4059418511179374671)
XLA Ops:
  0.6 1.1 %shard_map.67 = (f32[22,2,8,128]{3,2,1,0:T(8,128)S(1)}, f32[3,8,128]{2,1,0:T(8,128)S(1)}) custom-call(f32[19,2,8,128]{3,2,1,0:T(8,128)} %f_ref.1, f32[2,8,128]{2,1,0:T(8,128)} %por_ref.1, s32[2,8,128]{2,1,0:T(8,128)} %kind_ref.1, f32[2,8,128]{2,1,0:T(8,128)} %wgt_hbm.1), custom_call_target="tpu_custom_call" | custom-call | tf_op jit(solution)/shard_map/pallas_call | solution.py:463
  1.7 4.8 %collective-permute-start.1 = (f32[3,8,128]{2,1,0:T(8,128)S(1)}, f32[3,8,128]{2,1,0:T(8,128)S(1)}, u32[]{:S(2)}, u32[]{:S(2)}) collective-permute-start(f32[3,8,128]{2,1,0:T(8,128)S(1)} %get-tuple-element.18), channel_id=1, source_target_pairs={{0,256},{256,0},{512,768},{768,512},{1,257},{257,1},{513,769},{769... | collective-permute-start | bytes 36872 | tf_op jit(solution)/shard_map/ppermute | solution.py:448
  6.6 0.7 collective-permute-start
  7.2 0.4 collective-permute-done.1.even_ref
  7.6 0.0 collective-permute-done.odd_ref
  7.6 0.1 shard_map.68
  7.7 0.7 collective-permute-start.2
  8.4 5.6 %collective-permute-start.3 = (f32[144,128]{1,0:T(8,128)S(1)}, f32[144,128]{1,0:T(8,128)S(1)}, u32[]{:S(2)}, u32[]{:S(2)}) collective-permute-start(f32[144,128]{1,0:T(8,128)S(1)} %get-tuple-element.21), channel_id=1, source_target_pairs={{0,16},{16,0},{32,48},{48,32},{64,80},{80,64},{96,112},{112,96},{1... | collective-permute-start | bytes 221192 | tf_op jit(solution)/shard_map/ppermute | solution.py:448
  14.0 0.0 collective-permute-done.2.odd_ref
  14.0 1.7 %collective-permute-done.3.even_ref = f32[144,128]{1,0:T(8,128)S(1)} collective-permute-done((f32[144,128]{1,0:T(8,128)S(1)}, f32[144,128]{1,0:T(8,128)S(1)}, u32[]{:S(2)}, u32[]{:S(2)}) %collective-permute-start.3) | collective-permute-done | bytes 73760 | tf_op jit(solution)/shard_map/ppermute | solution.py:448
  15.7 0.1 shard_map.69
  15.8 5.8 %collective-permute-start.4 = (f32[24,2,8,128]{3,2,1,0:T(8,128)S(1)}, f32[24,2,8,128]{3,2,1,0:T(8,128)S(1)}, u32[]{:S(2)}, u32[]{:S(2)}) collective-permute-start(f32[24,2,8,128]{3,2,1,0:T(8,128)S(1)} %get-tuple-element.24), channel_id=1, source_target_pairs={{1,2},{2,1},{3,4},{4,3},{5,6},{6,5},{7,8},{8,7},{9,10},{10,9},{11,... | collective-permute-start | bytes 589832 | tf_op jit(solution)/shard_map/ppermute | solution.py:447
  21.6 9.6 %collective-permute-start.5 = (f32[24,2,8,128]{3,2,1,0:T(8,128)S(1)}, f32[24,2,8,128]{3,2,1,0:T(8,128)S(1)}, u32[]{:S(2)}, u32[]{:S(2)}) collective-permute-start(f32[24,2,8,128]{3,2,1,0:T(8,128)S(1)} %get-tuple-element.25), channel_id=1, source_target_pairs={{0,1},{1,0},{2,3},{3,2},{4,5},{5,4},{6,7},{7,6},{8,9},{9,8},{10,11... | collective-permute-start | bytes 589832 | tf_op jit(solution)/shard_map/ppermute | solution.py:448
  31.2 0.0 collective-permute-done.4.odd_ref
  31.2 1.0 %collective-permute-done.5.even_ref = f32[24,2,8,128]{3,2,1,0:T(8,128)S(1)} collective-permute-done((f32[24,2,8,128]{3,2,1,0:T(8,128)S(1)}, f32[24,2,8,128]{3,2,1,0:T(8,128)S(1)}, u32[]{:S(2)}, u32[]{:S(2)}) %collective-permute-start.5) | collective-permute-done | bytes 196640 | tf_op jit(solution)/shard_map/ppermute | solution.py:448
  32.3 0.0 copy-start
  32.3 2.1 %shard_map.70 = (f32[5,4,16,256]{3,2,1,0:T(8,128)S(1)}, f32[7,2,8,128]{3,2,1,0:T(8,128)S(1)}, f32[16,1,128]{2,1,0:T(1,128)S(1)}) custom-call(f32[22,2,2,8,128]{4,3,2,1,0:T(8,128)S(1)} %get-tuple-element.22.wide_ref, f32[3,2,8,128]{3,2,1,0:T(8,128)S(1)} %get-tuple-element.23.side_ref, f32[24,2,8,128]{3,2,1,0:T(8,128)S(1)} %collective-permute-done.4.odd_ref, ...), custom_call_target="tpu_custom_call" | custom-call | tf_op jit(solution)/shard_map/pallas_call | solution.py:486
  34.4 8.8 %all_to_all.10.in_ref = f32[16,1,128]{2,1,0:T(1,128)S(1)} all-to-all(f32[16,1,128]{2,1,0:T(1,128)S(1)} %get-tuple-element.30), channel_id=1, replica_groups={{15,14,13,12,11,10,9,8,7,6,5,4,3,2,1,0},{31,30,29,28,27,26,25,24,23,22,..., dimensions={0} | all-to-all | bytes 16384 | tf_op jit(solution)/shard_map/all_to_all | solution.py:493
  43.2 0.6 shard_map.72
  43.8 0.0 copy-start.1
  43.8 0.0 copy-start.2
  43.8 26.5 %all-to-all-start.1 = ((f32[64,1,128]{2,1,0:T(1,128)}), f32[64,1,128]{2,1,0:T(1,128)S(1)}, u32[]{:S(2)}, u32[]{:S(2)}) async-start(f32[64,1,128]{2,1,0:T(1,128)} %shard_map.72), calls=%async_computation.1 | async-start | bytes 65536 | tf_op jit(solution)/shard_map/all_to_all | solution.py:495
  70.3 3.3 %collective-permute-start.7 = (f32[7,2,8,128]{3,2,1,0:T(8,128)S(1)}, f32[7,2,8,128]{3,2,1,0:T(8,128)S(1)}, u32[]{:S(2)}, u32[]{:S(2)}) collective-permute-start(f32[7,2,8,128]{3,2,1,0:T(8,128)S(1)} %get-tuple-element.26.flow_ref), channel_id=1, source_target_pairs={{1,2},{2,1},{3,4},{4,3},{5,6},{6,5},{7,8},{8,7},{9,10},{10,9},{11,... | collective-permute-start | bytes 172040 | tf_op jit(solution)/shard_map/ppermute | solution.py:445
  73.6 1.9 %collective-permute-start.6 = (f32[7,2,8,128]{3,2,1,0:T(8,128)S(1)}, f32[7,2,8,128]{3,2,1,0:T(8,128)S(1)}, u32[]{:S(2)}, u32[]{:S(2)}) collective-permute-start(f32[7,2,8,128]{3,2,1,0:T(8,128)S(1)} %get-tuple-element.26.flow_ref), channel_id=1, source_target_pairs={{0,1},{1,0},{2,3},{3,2},{4,5},{5,4},{6,7},{7,6},{8,9},{9,8},{10,11... | collective-permute-start | bytes 172040 | tf_op jit(solution)/shard_map/ppermute | solution.py:444
  75.5 0.5 collective-permute-done.7.odd_ref
  76.1 0.7 collective-permute-done.6.even_ref
  76.8 0.0 copy-done
  76.8 0.0 copy-done.1
  76.8 0.0 copy-done.2
  76.8 1.2 %shard_map.71 = (f32[19,2,8,128]{3,2,1,0:T(8,128)}, f32[2,8,128]{2,1,0:T(8,128)}) custom-call(f32[7,2,8,128]{3,2,1,0:T(8,128)S(1)} %get-tuple-element.26.flow_ref, f32[7,2,8,128]{3,2,1,0:T(8,128)S(1)} %collective-permute-done.6.even_ref, f32[7,2,8,128]{3,2,1,0:T(8,128)S(1)} %collective-permute-done.7.odd_ref, ...), custom_call_target="tpu_custom_call" | custom-call | tf_op jit(solution)/shard_map/pallas_call | solution.py:499
  78.0 0.4 all-to-all-done.1
  78.4 0.7 reduce_sum.9
Async XLA Ops:
  1.7 5.9 %collective-permute-start.1 = (f32[3,8,128]{2,1,0:T(8,128)S(1)}, f32[3,8,128]{2,1,0:T(8,128)S(1)}, u32[]{:S(2)}, u32[]{:S(2)}) collective-permute-start(f32[3,8,128]{2,1,0:T(8,128)S(1)} %get-tuple-element.18), channel_id=1, source_target_pairs={{0,256},{256,0},{512,768},{768,512},{1,257},{257,1},{513,769},{769... | collective-permute-start | bytes 36872 | tf_op jit(solution)/shard_map/ppermute | solution.py:448
  6.6 1.1 %collective-permute-start = (f32[3,8,128]{2,1,0:T(8,128)S(1)}, f32[3,8,128]{2,1,0:T(8,128)S(1)}, u32[]{:S(2)}, u32[]{:S(2)}) collective-permute-start(f32[3,8,128]{2,1,0:T(8,128)S(1)} %get-tuple-element.18), channel_id=1, source_target_pairs={{256,512},{512,256},{257,513},{513,257},{258,514},{514,258},{259,5... | collective-permute-start | bytes 36872 | tf_op jit(solution)/shard_map/ppermute | solution.py:447
  7.7 6.3 %collective-permute-start.2 = (f32[144,128]{1,0:T(8,128)S(1)}, f32[144,128]{1,0:T(8,128)S(1)}, u32[]{:S(2)}, u32[]{:S(2)}) collective-permute-start(f32[144,128]{1,0:T(8,128)S(1)} %get-tuple-element.20), channel_id=1, source_target_pairs={{16,32},{32,16},{48,64},{64,48},{80,96},{96,80},{112,128},{128,112... | collective-permute-start | bytes 221192 | tf_op jit(solution)/shard_map/ppermute | solution.py:447
  8.4 7.3 %collective-permute-start.3 = (f32[144,128]{1,0:T(8,128)S(1)}, f32[144,128]{1,0:T(8,128)S(1)}, u32[]{:S(2)}, u32[]{:S(2)}) collective-permute-start(f32[144,128]{1,0:T(8,128)S(1)} %get-tuple-element.21), channel_id=1, source_target_pairs={{0,16},{16,0},{32,48},{48,32},{64,80},{80,64},{96,112},{112,96},{1... | collective-permute-start | bytes 221192 | tf_op jit(solution)/shard_map/ppermute | solution.py:448
  15.8 15.4 %collective-permute-start.4 = (f32[24,2,8,128]{3,2,1,0:T(8,128)S(1)}, f32[24,2,8,128]{3,2,1,0:T(8,128)S(1)}, u32[]{:S(2)}, u32[]{:S(2)}) collective-permute-start(f32[24,2,8,128]{3,2,1,0:T(8,128)S(1)} %get-tuple-element.24), channel_id=1, source_target_pairs={{1,2},{2,1},{3,4},{4,3},{5,6},{6,5},{7,8},{8,7},{9,10},{10,9},{11,... | collective-permute-start | bytes 589832 | tf_op jit(solution)/shard_map/ppermute | solution.py:447
  21.6 10.6 %collective-permute-start.5 = (f32[24,2,8,128]{3,2,1,0:T(8,128)S(1)}, f32[24,2,8,128]{3,2,1,0:T(8,128)S(1)}, u32[]{:S(2)}, u32[]{:S(2)}) collective-permute-start(f32[24,2,8,128]{3,2,1,0:T(8,128)S(1)} %get-tuple-element.25), channel_id=1, source_target_pairs={{0,1},{1,0},{2,3},{3,2},{4,5},{5,4},{6,7},{7,6},{8,9},{9,8},{10,11... | collective-permute-start | bytes 589832 | tf_op jit(solution)/shard_map/ppermute | solution.py:448
  32.3 44.5 %copy-start = (f32[19,2,8,128]{3,2,1,0:T(8,128)S(1)}, f32[19,2,8,128]{3,2,1,0:T(8,128)}, u32[]{:S(2)}) copy-start(f32[19,2,8,128]{3,2,1,0:T(8,128)} %f_ref.1) | copy-start | bytes 466948
  43.8 33.0 %copy-start.1 = (f32[2,8,128]{2,1,0:T(8,128)S(1)}, f32[2,8,128]{2,1,0:T(8,128)}, u32[]{:S(2)}) copy-start(f32[2,8,128]{2,1,0:T(8,128)} %por_ref.1) | copy-start | bytes 24580
  43.8 33.0 %copy-start.2 = (s32[2,8,128]{2,1,0:T(8,128)S(1)}, s32[2,8,128]{2,1,0:T(8,128)}, u32[]{:S(2)}) copy-start(s32[2,8,128]{2,1,0:T(8,128)} %kind_ref.1) | copy-start | bytes 24580
  43.8 34.6 %all-to-all-start.1 = ((f32[64,1,128]{2,1,0:T(1,128)}), f32[64,1,128]{2,1,0:T(1,128)S(1)}, u32[]{:S(2)}, u32[]{:S(2)}) async-start(f32[64,1,128]{2,1,0:T(1,128)} %shard_map.72), calls=%async_computation.1 | async-start | bytes 65536 | tf_op jit(solution)/shard_map/all_to_all | solution.py:495
  70.3 5.8 %collective-permute-start.7 = (f32[7,2,8,128]{3,2,1,0:T(8,128)S(1)}, f32[7,2,8,128]{3,2,1,0:T(8,128)S(1)}, u32[]{:S(2)}, u32[]{:S(2)}) collective-permute-start(f32[7,2,8,128]{3,2,1,0:T(8,128)S(1)} %get-tuple-element.26.flow_ref), channel_id=1, source_target_pairs={{1,2},{2,1},{3,4},{4,3},{5,6},{6,5},{7,8},{8,7},{9,10},{10,9},{11,... | collective-permute-start | bytes 172040 | tf_op jit(solution)/shard_map/ppermute | solution.py:445
  73.6 3.1 %collective-permute-start.6 = (f32[7,2,8,128]{3,2,1,0:T(8,128)S(1)}, f32[7,2,8,128]{3,2,1,0:T(8,128)S(1)}, u32[]{:S(2)}, u32[]{:S(2)}) collective-permute-start(f32[7,2,8,128]{3,2,1,0:T(8,128)S(1)} %get-tuple-element.26.flow_ref), channel_id=1, source_target_pairs={{0,1},{1,0},{2,3},{3,2},{4,5},{5,4},{6,7},{7,6},{8,9},{9,8},{10,11... | collective-permute-start | bytes 172040 | tf_op jit(solution)/shard_map/ppermute | solution.py:444

commit v2 on v0

--- a/solution.py
+++ b/solution.py
@@ -489,7 +489,9 @@
         [(19,) + field],
     )(wide, side, *swap("gz", to_even, to_odd))
     flow_odd, flow_even = swap("gz", flow, flow, True)
-    part = lax.all_to_all(part, "gz", 0, 0, tiled=True)
+    falling = list(range(group))[::-1]
+    turned = [falling[group // 8 :] + falling[: group // 8]]
+    part = lax.all_to_all(part, "gz", 0, 0, axis_index_groups=turned, tiled=True)
     part = call(spread_kernel, [(plane, 1, XS)])(part)
     part = lax.all_to_all(
         part, ("gx", "gy", "gz"), 0, 0, axis_index_groups=columns(), tiled=True

time: 81.9 us -> 78.6 us (0.960)
  starting transfers between devices: 60.1 us -> 57.9 us
  blocking collectives: 9.82 us -> 8.79 us
    all_to_all x1, starting transfers between devices: 27.8 us -> 25.6 us  [per_device(): lax.all_to_all(part, ('gx', 'gy', 'gz'), 0, 0, axis_index_groups=columns(...]
    all_to_all x1, blocking collectives: 9.82 us -> 8.79 us  [per_device(): lax.all_to_all(part, 'gz', 0, 0, axis_index_groups=turned, tiled=True)]
  transfers between devices with their start and end apart: 9 -> 9, of which waited for: 6 -> 6; matrix products, arithmetic and copies ran while one was open for 0% -> 0% of each run, Pallas kernels for 1% -> 2%
where the time goes in v2:
time: 78.6 us; the launch traced here: 78.2 us
  starting transfers between devices  57.9 us (74%)
  blocking collectives  8.79 us (11%)
  Pallas kernels  5.23 us (7%)
  waiting for transfers between devices  4.78 us (6%)
    all_to_all x1, starting transfers between devices, per_device(): lax.all_to_all(part, ('gx', 'gy', 'gz'), 0, 0, axis_index_groups=columns(...  25.6 us
    ppermute x4, starting transfers between devices, swap(): even = lax.ppermute(to_even, axis, partners(0))  21.9 us
    ppermute x4, starting transfers between devices, swap(): odd = lax.ppermute(to_odd, axis, partners(1))  10.5 us
    all_to_all x1, blocking collectives, per_device(): lax.all_to_all(part, 'gz', 0, 0, axis_index_groups=turned, tiled=True)  8.79 us
    ppermute x4, waiting for transfers between devices, swap(): even = lax.ppermute(to_even, axis, partners(0))  3.85 us
    pallas_call x1, Pallas kernels, per_device(): call(functools.partial(forward_kernel, 0.5 / cells), [(5,) + field, (3 *...  2.11 us
  transfers between devices with their start and end apart: 9, of which 6 were waited for; matrix products, arithmetic and copies ran while one was open for 0% of the time, Pallas kernels for 2%

profile of v2, /device:TPU:1, one launch (start us, length us, event | category | flops | bytes accessed | tf_op | source)
XLA Modules:
  0.0 78.2 jit_solution(453419340831590350)
XLA Ops:
  0.6 1.1 %shard_map.67 = (f32[22,2,8,128]{3,2,1,0:T(8,128)S(1)}, f32[3,8,128]{2,1,0:T(8,128)S(1)}) custom-call(f32[19,2,8,128]{3,2,1,0:T(8,128)} %f_ref.1, f32[2,8,128]{2,1,0:T(8,128)} %por_ref.1, s32[2,8,128]{2,1,0:T(8,128)} %kind_ref.1, f32[2,8,128]{2,1,0:T(8,128)} %wgt_hbm.1), custom_call_target="tpu_custom_call" | custom-call | tf_op jit(solution)/shard_map/pallas_call | solution.py:463
  1.7 4.8 %collective-permute-start.1 = (f32[3,8,128]{2,1,0:T(8,128)S(1)}, f32[3,8,128]{2,1,0:T(8,128)S(1)}, u32[]{:S(2)}, u32[]{:S(2)}) collective-permute-start(f32[3,8,128]{2,1,0:T(8,128)S(1)} %get-tuple-element.18), channel_id=1, source_target_pairs={{0,256},{256,0},{512,768},{768,512},{1,257},{257,1},{513,769},{769... | collective-permute-start | bytes 36872 | tf_op jit(solution)/shard_map/ppermute | solution.py:448
  6.6 0.7 collective-permute-start
  7.2 0.4 collective-permute-done.1.even_ref
  7.6 0.0 collective-permute-done.odd_ref
  7.6 0.1 shard_map.68
  7.7 0.7 collective-permute-start.2
  8.4 5.6 %collective-permute-start.3 = (f32[144,128]{1,0:T(8,128)S(1)}, f32[144,128]{1,0:T(8,128)S(1)}, u32[]{:S(2)}, u32[]{:S(2)}) collective-permute-start(f32[144,128]{1,0:T(8,128)S(1)} %get-tuple-element.21), channel_id=1, source_target_pairs={{0,16},{16,0},{32,48},{48,32},{64,80},{80,64},{96,112},{112,96},{1... | collective-permute-start | bytes 221192 | tf_op jit(solution)/shard_map/ppermute | solution.py:448
  14.0 0.0 collective-permute-done.2.odd_ref
  14.0 1.7 %collective-permute-done.3.even_ref = f32[144,128]{1,0:T(8,128)S(1)} collective-permute-done((f32[144,128]{1,0:T(8,128)S(1)}, f32[144,128]{1,0:T(8,128)S(1)}, u32[]{:S(2)}, u32[]{:S(2)}) %collective-permute-start.3) | collective-permute-done | bytes 73760 | tf_op jit(solution)/shard_map/ppermute | solution.py:448
  15.7 0.1 shard_map.69
  15.8 5.8 %collective-permute-start.4 = (f32[24,2,8,128]{3,2,1,0:T(8,128)S(1)}, f32[24,2,8,128]{3,2,1,0:T(8,128)S(1)}, u32[]{:S(2)}, u32[]{:S(2)}) collective-permute-start(f32[24,2,8,128]{3,2,1,0:T(8,128)S(1)} %get-tuple-element.24), channel_id=1, source_target_pairs={{1,2},{2,1},{3,4},{4,3},{5,6},{6,5},{7,8},{8,7},{9,10},{10,9},{11,... | collective-permute-start | bytes 589832 | tf_op jit(solution)/shard_map/ppermute | solution.py:447
  21.6 9.6 %collective-permute-start.5 = (f32[24,2,8,128]{3,2,1,0:T(8,128)S(1)}, f32[24,2,8,128]{3,2,1,0:T(8,128)S(1)}, u32[]{:S(2)}, u32[]{:S(2)}) collective-permute-start(f32[24,2,8,128]{3,2,1,0:T(8,128)S(1)} %get-tuple-element.25), channel_id=1, source_target_pairs={{0,1},{1,0},{2,3},{3,2},{4,5},{5,4},{6,7},{7,6},{8,9},{9,8},{10,11... | collective-permute-start | bytes 589832 | tf_op jit(solution)/shard_map/ppermute | solution.py:448
  31.2 0.0 collective-permute-done.4.odd_ref
  31.2 1.0 %collective-permute-done.5.even_ref = f32[24,2,8,128]{3,2,1,0:T(8,128)S(1)} collective-permute-done((f32[24,2,8,128]{3,2,1,0:T(8,128)S(1)}, f32[24,2,8,128]{3,2,1,0:T(8,128)S(1)}, u32[]{:S(2)}, u32[]{:S(2)}) %collective-permute-start.5) | collective-permute-done | bytes 196640 | tf_op jit(solution)/shard_map/ppermute | solution.py:448
  32.3 0.0 copy-start
  32.3 2.1 %shard_map.70 = (f32[5,4,16,256]{3,2,1,0:T(8,128)S(1)}, f32[7,2,8,128]{3,2,1,0:T(8,128)S(1)}, f32[16,1,128]{2,1,0:T(1,128)S(1)}) custom-call(f32[22,2,2,8,128]{4,3,2,1,0:T(8,128)S(1)} %get-tuple-element.22.wide_ref, f32[3,2,8,128]{3,2,1,0:T(8,128)S(1)} %get-tuple-element.23.side_ref, f32[24,2,8,128]{3,2,1,0:T(8,128)S(1)} %collective-permute-done.4.odd_ref, ...), custom_call_target="tpu_custom_call" | custom-call | tf_op jit(solution)/shard_map/pallas_call | solution.py:486
  34.4 8.8 %all_to_all.10.in_ref = f32[16,1,128]{2,1,0:T(1,128)S(1)} all-to-all(f32[16,1,128]{2,1,0:T(1,128)S(1)} %get-tuple-element.30), channel_id=1, replica_groups={{13,12,11,10,9,8,7,6,5,4,3,2,1,0,15,14},{29,28,27,26,25,24,23,22,21,20,..., dimensions={0} | all-to-all | bytes 16384 | tf_op jit(solution)/shard_map/all_to_all | solution.py:494
  43.2 0.6 shard_map.72
  43.8 0.0 copy-start.1
  43.8 0.0 copy-start.2
  43.8 25.6 %all-to-all-start.1 = ((f32[64,1,128]{2,1,0:T(1,128)}), f32[64,1,128]{2,1,0:T(1,128)S(1)}, u32[]{:S(2)}, u32[]{:S(2)}) async-start(f32[64,1,128]{2,1,0:T(1,128)} %shard_map.72), calls=%async_computation.1 | async-start | bytes 65536 | tf_op jit(solution)/shard_map/all_to_all | solution.py:496
  69.4 3.3 %collective-permute-start.7 = (f32[7,2,8,128]{3,2,1,0:T(8,128)S(1)}, f32[7,2,8,128]{3,2,1,0:T(8,128)S(1)}, u32[]{:S(2)}, u32[]{:S(2)}) collective-permute-start(f32[7,2,8,128]{3,2,1,0:T(8,128)S(1)} %get-tuple-element.26.flow_ref), channel_id=1, source_target_pairs={{1,2},{2,1},{3,4},{4,3},{5,6},{6,5},{7,8},{8,7},{9,10},{10,9},{11,... | collective-permute-start | bytes 172040 | tf_op jit(solution)/shard_map/ppermute | solution.py:445
  72.8 1.9 %collective-permute-start.6 = (f32[7,2,8,128]{3,2,1,0:T(8,128)S(1)}, f32[7,2,8,128]{3,2,1,0:T(8,128)S(1)}, u32[]{:S(2)}, u32[]{:S(2)}) collective-permute-start(f32[7,2,8,128]{3,2,1,0:T(8,128)S(1)} %get-tuple-element.26.flow_ref), channel_id=1, source_target_pairs={{0,1},{1,0},{2,3},{3,2},{4,5},{5,4},{6,7},{7,6},{8,9},{9,8},{10,11... | collective-permute-start | bytes 172040 | tf_op jit(solution)/shard_map/ppermute | solution.py:444
  74.7 0.5 collective-permute-done.7.odd_ref
  75.2 0.7 collective-permute-done.6.even_ref
  75.9 0.0 copy-done
  75.9 0.0 copy-done.1
  75.9 0.0 copy-done.2
  75.9 1.2 %shard_map.71 = (f32[19,2,8,128]{3,2,1,0:T(8,128)}, f32[2,8,128]{2,1,0:T(8,128)}) custom-call(f32[7,2,8,128]{3,2,1,0:T(8,128)S(1)} %get-tuple-element.26.flow_ref, f32[7,2,8,128]{3,2,1,0:T(8,128)S(1)} %collective-permute-done.6.even_ref, f32[7,2,8,128]{3,2,1,0:T(8,128)S(1)} %collective-permute-done.7.odd_ref, ...), custom_call_target="tpu_custom_call" | custom-call | tf_op jit(solution)/shard_map/pallas_call | solution.py:500
  77.1 0.4 all-to-all-done.1
  77.5 0.7 reduce_sum.9
Async XLA Ops:
  1.7 5.9 %collective-permute-start.1 = (f32[3,8,128]{2,1,0:T(8,128)S(1)}, f32[3,8,128]{2,1,0:T(8,128)S(1)}, u32[]{:S(2)}, u32[]{:S(2)}) collective-permute-start(f32[3,8,128]{2,1,0:T(8,128)S(1)} %get-tuple-element.18), channel_id=1, source_target_pairs={{0,256},{256,0},{512,768},{768,512},{1,257},{257,1},{513,769},{769... | collective-permute-start | bytes 36872 | tf_op jit(solution)/shard_map/ppermute | solution.py:448
  6.6 1.1 %collective-permute-start = (f32[3,8,128]{2,1,0:T(8,128)S(1)}, f32[3,8,128]{2,1,0:T(8,128)S(1)}, u32[]{:S(2)}, u32[]{:S(2)}) collective-permute-start(f32[3,8,128]{2,1,0:T(8,128)S(1)} %get-tuple-element.18), channel_id=1, source_target_pairs={{256,512},{512,256},{257,513},{513,257},{258,514},{514,258},{259,5... | collective-permute-start | bytes 36872 | tf_op jit(solution)/shard_map/ppermute | solution.py:447
  7.7 6.3 %collective-permute-start.2 = (f32[144,128]{1,0:T(8,128)S(1)}, f32[144,128]{1,0:T(8,128)S(1)}, u32[]{:S(2)}, u32[]{:S(2)}) collective-permute-start(f32[144,128]{1,0:T(8,128)S(1)} %get-tuple-element.20), channel_id=1, source_target_pairs={{16,32},{32,16},{48,64},{64,48},{80,96},{96,80},{112,128},{128,112... | collective-permute-start | bytes 221192 | tf_op jit(solution)/shard_map/ppermute | solution.py:447
  8.4 7.3 %collective-permute-start.3 = (f32[144,128]{1,0:T(8,128)S(1)}, f32[144,128]{1,0:T(8,128)S(1)}, u32[]{:S(2)}, u32[]{:S(2)}) collective-permute-start(f32[144,128]{1,0:T(8,128)S(1)} %get-tuple-element.21), channel_id=1, source_target_pairs={{0,16},{16,0},{32,48},{48,32},{64,80},{80,64},{96,112},{112,96},{1... | collective-permute-start | bytes 221192 | tf_op jit(solution)/shard_map/ppermute | solution.py:448
  15.8 15.4 %collective-permute-start.4 = (f32[24,2,8,128]{3,2,1,0:T(8,128)S(1)}, f32[24,2,8,128]{3,2,1,0:T(8,128)S(1)}, u32[]{:S(2)}, u32[]{:S(2)}) collective-permute-start(f32[24,2,8,128]{3,2,1,0:T(8,128)S(1)} %get-tuple-element.24), channel_id=1, source_target_pairs={{1,2},{2,1},{3,4},{4,3},{5,6},{6,5},{7,8},{8,7},{9,10},{10,9},{11,... | collective-permute-start | bytes 589832 | tf_op jit(solution)/shard_map/ppermute | solution.py:447
  21.6 10.6 %collective-permute-start.5 = (f32[24,2,8,128]{3,2,1,0:T(8,128)S(1)}, f32[24,2,8,128]{3,2,1,0:T(8,128)S(1)}, u32[]{:S(2)}, u32[]{:S(2)}) collective-permute-start(f32[24,2,8,128]{3,2,1,0:T(8,128)S(1)} %get-tuple-element.25), channel_id=1, source_target_pairs={{0,1},{1,0},{2,3},{3,2},{4,5},{5,4},{6,7},{7,6},{8,9},{9,8},{10,11... | collective-permute-start | bytes 589832 | tf_op jit(solution)/shard_map/ppermute | solution.py:448
  32.3 43.6 %copy-start = (f32[19,2,8,128]{3,2,1,0:T(8,128)S(1)}, f32[19,2,8,128]{3,2,1,0:T(8,128)}, u32[]{:S(2)}) copy-start(f32[19,2,8,128]{3,2,1,0:T(8,128)} %f_ref.1) | copy-start | bytes 466948
  43.8 32.1 %copy-start.1 = (f32[2,8,128]{2,1,0:T(8,128)S(1)}, f32[2,8,128]{2,1,0:T(8,128)}, u32[]{:S(2)}) copy-start(f32[2,8,128]{2,1,0:T(8,128)} %por_ref.1) | copy-start | bytes 24580
  43.8 32.1 %copy-start.2 = (s32[2,8,128]{2,1,0:T(8,128)S(1)}, s32[2,8,128]{2,1,0:T(8,128)}, u32[]{:S(2)}) copy-start(s32[2,8,128]{2,1,0:T(8,128)} %kind_ref.1) | copy-start | bytes 24580
  43.8 33.7 %all-to-all-start.1 = ((f32[64,1,128]{2,1,0:T(1,128)}), f32[64,1,128]{2,1,0:T(1,128)S(1)}, u32[]{:S(2)}, u32[]{:S(2)}) async-start(f32[64,1,128]{2,1,0:T(1,128)} %shard_map.72), calls=%async_computation.1 | async-start | bytes 65536 | tf_op jit(solution)/shard_map/all_to_all | solution.py:496
  69.4 5.8 %collective-permute-start.7 = (f32[7,2,8,128]{3,2,1,0:T(8,128)S(1)}, f32[7,2,8,128]{3,2,1,0:T(8,128)S(1)}, u32[]{:S(2)}, u32[]{:S(2)}) collective-permute-start(f32[7,2,8,128]{3,2,1,0:T(8,128)S(1)} %get-tuple-element.26.flow_ref), channel_id=1, source_target_pairs={{1,2},{2,1},{3,4},{4,3},{5,6},{6,5},{7,8},{8,7},{9,10},{10,9},{11,... | collective-permute-start | bytes 172040 | tf_op jit(solution)/shard_map/ppermute | solution.py:445
  72.8 3.1 %collective-permute-start.6 = (f32[7,2,8,128]{3,2,1,0:T(8,128)S(1)}, f32[7,2,8,128]{3,2,1,0:T(8,128)S(1)}, u32[]{:S(2)}, u32[]{:S(2)}) collective-permute-start(f32[7,2,8,128]{3,2,1,0:T(8,128)S(1)} %get-tuple-element.26.flow_ref), channel_id=1, source_target_pairs={{0,1},{1,0},{2,3},{3,2},{4,5},{5,4},{6,7},{7,6},{8,9},{9,8},{10,11... | collective-permute-start | bytes 172040 | tf_op jit(solution)/shard_map/ppermute | solution.py:444
